TPU v7x, 128 devices: a whole 4x4x4 slice. The times are simulated.
128 devices in a mesh: ctx: 32 (over z, x_hi, y), head: 4 (over x_lo, core).
Axes of the slice: x: 4 (x_hi: 2, x_lo: 2; x = x_hi * 2 + x_lo), y: 4, z: 4, core: 2. Of those that a mesh axis runs over, the one named last changes fastest.
Arguments:
- queries: bfloat16 [16384, 4096], P('ctx', 'head'), may hold values from -140 to 140
- keys: bfloat16 [16384, 1024], P('ctx', 'head'), may hold values from -10 to 10
- values: bfloat16 [16384, 1024], P('ctx', 'head'), may hold values from -6 to 6
- selected: int32 [32, 3], P('ctx'), may hold values from 0 to 31, as said below
- out_weight: bfloat16 [4096, 4096], P('head'), may hold values from -0.09375 to 0.09375
- out_grad: bfloat16 [16384, 4096], P('ctx', 'head'), may hold values from -6 to 6
Outputs:
- projected: bfloat16 [16384, 4096], P('ctx', 'head')
- query_grad: bfloat16 [16384, 4096], P('ctx', 'head')
- key_grad: bfloat16 [16384, 1024], P('ctx', 'head')
- value_grad: bfloat16 [16384, 1024], P('ctx', 'head')
Inputs may be any that keep to these rules, and one draw needn't show every extreme that they name: selected[b, 0] = b. Each other entry is either b (an unused slot) or a distinct earlier block at most 4 blocks before b.
All inputs are finite; a program needn't handle non-finite values.
Results may differ from a plain program's by a relative error of at most 0.034.
Values may be sent and summed in bfloat16 or wider, within the bound.
A program may use at most 192 MiB of HBM per device.

v0:
```python
import functools
import math

import jax
import jax.numpy as jnp
from jax import lax
from jax.experimental import pallas as pl
from jax.experimental.pallas import tpu as pltpu
from jax.sharding import PartitionSpec as P

HD = 128
BLOCK = 512
HALF = BLOCK // 2
WIDTH = 1024
GROUP = 4
KV = 2
ROW = 4
MESH = pl.DeviceIdType.MESH
SCALE = 1.0 / math.sqrt(HD)
EXP2_SCALE = SCALE * math.log2(math.e)
BF16 = jnp.bfloat16
F32 = jnp.float32
OG_CUTS = 2
OG_ROWS = BLOCK // OG_CUTS


def nn(a, b):
    return lax.dot_general(a, b, (((1,), (0,)), ((), ())), preferred_element_type=F32)


def nt(a, b):
    return lax.dot_general(a, b, (((1,), (1,)), ((), ())), preferred_element_type=F32)


def kernel(
    sel, q_hbm, k_hbm, v_hbm, w_hbm, og_hbm,
    proj_hbm, dq_hbm, dk_hbm, dv_hbm,
    own, win0, win1, vt, kt, qv, wv, ogb, dot_, ot, ob, rl, eb, sb, acc,
    gs0, gs1, gr0, gr1, gxs, gxr, pcs, pcr, pxs, pxr, pown, dqv, dkv_out,
    lsem, osem, xs, xr, ds_, dr, ocs, ocr, oxs, oxr, ofs, ofr, pcss, pcrs, pxss, pxrs, bds, bdr, bxs, bxr,
):
    win = (win0, win1)
    gs = (gs0, gs1)
    gr = (gr0, gr1)
    ctx = lax.axis_index("ctx")
    head = lax.axis_index("head")
    y = lax.rem(ctx, ROW)
    row_start = ctx - y
    following = lax.rem(ctx + ROW, 32)
    preceding = lax.rem(ctx + 32 - ROW, 32)
    chip = head // 2
    core = lax.rem(head, 2)
    other_core = chip * 2 + 1 - core
    other_chip = (1 - chip) * 2 + core
    diagonal = (1 - chip) * 2 + 1 - core

    def peer(k):
        return row_start + lax.rem(y + k, ROW)

    def remote(src, dst, ss, rs, c, h):
        return pltpu.make_async_remote_copy(
            src_ref=src, dst_ref=dst, send_sem=ss, recv_sem=rs, device_id=(c, h), device_id_type=MESH
        )

    kv_in = []
    for g in range(KV):
        cols = pl.ds(g * HD, HD)
        kv_in.append(
            (
                pltpu.make_async_copy(k_hbm.at[:, cols], own.at[g, 0], lsem.at[2 * g]),
                pltpu.make_async_copy(v_hbm.at[:, cols], own.at[g, 1], lsem.at[2 * g + 1]),
            )
        )
        kv_in[g][0].start()
        kv_in[g][1].start()
    og_in = pltpu.make_async_copy(og_hbm, ogb.at[head], lsem.at[4])
    og_in.start()
    w_in = pltpu.make_async_copy(w_hbm, wv, lsem.at[5])
    w_in.start()
    q_in = pltpu.make_async_copy(q_hbm, qv, lsem.at[6])
    q_in.start()

    barrier = pltpu.get_barrier_semaphore()
    for c, h in (
        (following, head), (preceding, head), (peer(1), head), (peer(2), head), (peer(3), head),
        (ctx, other_core), (ctx, other_chip),
    ):
        pl.semaphore_signal(barrier, inc=1, device_id=(c, h), device_id_type=MESH)
    pl.semaphore_wait(barrier, 7)

    cross = [
        remote(own.at[g], win[g].at[y], xs.at[g], xr.at[g], following, head) for g in range(KV)
    ]
    serve_own = [
        [remote(own.at[g], win[g].at[y], ds_.at[g, k - 1], dr.at[g, k - 1], peer(k), head) for k in (1, 2, 3)]
        for g in range(KV)
    ]
    serve_prev = [
        [remote(win[g].at[y], win[g].at[y], ds_.at[g, k - 1], dr.at[g, k - 1], peer(k), head) for k in (1, 2, 3)]
        for g in range(KV)
    ]
    for g in range(KV):
        kv_in[g][0].wait()
        kv_in[g][1].wait()
        cross[g].start()
        for k in (1, 3, 2):
            pl.when(y + k < ROW)(serve_own[g][k - 1].start)

    og_in.wait()
    og_core = remote(ogb.at[head], ogb.at[head], ocs.at[0], ocr.at[0], ctx, other_core)
    og_core.start()
    og_chip = []
    og_pass = []
    for i in range(OG_CUTS):
        rows = pl.ds(i * OG_ROWS, OG_ROWS)
        og_chip.append(
            remote(ogb.at[head, rows], ogb.at[head, rows], oxs.at[i], oxr.at[i], ctx, other_chip)
        )
        og_pass.append(
            remote(ogb.at[other_chip, rows], ogb.at[other_chip, rows], ofs.at[i], ofr.at[i], ctx, other_core)
        )

    def grad_block(block, first):
        cols = pl.ds(pl.multiple_of(block * WIDTH, WIDTH), WIDTH)

        def step(i, _):
            rows = pl.ds(pl.multiple_of(i * 256, 256), 256)
            part = nt(wv[rows, cols], ogb[block])
            dot_[rows, :] = part if first else dot_[rows, :] + part
            return 0

        lax.fori_loop(0, WIDTH // 256, step, 0)

    w_in.wait()
    grad_block(head, True)

    for g in range(KV):
        cross[g].wait_recv()
        for k in (3, 1, 2):
            pl.when(y + k >= ROW)(serve_prev[g][k - 1].start)
        og_chip[g].start()
        if g == 0:
            og_core.wait_recv()
            grad_block(other_core, False)

    sel1 = sel[0, 1]
    sel2 = sel[0, 2]
    col1 = lax.rem(sel1, ROW)
    col2 = lax.rem(sel2, ROW)
    live1 = sel1 != ctx
    live2 = sel2 != ctx

    key_pos = lax.broadcasted_iota(jnp.int32, (HALF, BLOCK), 0)
    query_pos = lax.broadcasted_iota(jnp.int32, (HALF, BLOCK), 1)

    def forward(g):
        w_ = win[g]
        vt[0] = own[g, 1].T
        vt[1] = w_[col1, 1].T
        vt[2] = w_[col2, 1].T

        def one_head(r, _):
            hh = g * GROUP + r
            hcols = pl.ds(pl.multiple_of(hh * HD, HD), HD)
            q = qv[:, hcols]
            s = nt(own[g, 0, :HALF], q)
            s = jnp.where(key_pos <= query_pos, s, -1e30)
            sb[0:HALF, :] = s
            top = jnp.max(s, axis=0, keepdims=True)
            s = nt(own[g, 0, HALF:], q[HALF:])
            s = jnp.where((key_pos <= query_pos)[:, :HALF], s, -1e30)
            sb[HALF:BLOCK, HALF:] = s
            top = jnp.concatenate(
                [top[:, :HALF], jnp.maximum(top[:, HALF:], jnp.max(s, axis=0, keepdims=True))], axis=1
            )
            for j, (col, live) in enumerate(((col1, live1), (col2, live2))):
                for half in range(2):
                    s = nt(w_[col, 0, half * HALF : (half + 1) * HALF], q)
                    sb[BLOCK * (j + 1) + half * HALF : BLOCK * (j + 1) + (half + 1) * HALF, :] = s
                    top = jnp.maximum(top, jnp.where(live, jnp.max(s, axis=0, keepdims=True), -1e30))
            shift = top * EXP2_SCALE
            e = jnp.exp2(sb[0:HALF, :] * EXP2_SCALE - shift)
            total = jnp.sum(e, axis=0, keepdims=True)
            e = e.astype(BF16)
            eb[hh, 0:HALF, :] = e
            out = nn(vt[0, :, :HALF], e)
            e = jnp.exp2(sb[HALF:BLOCK, HALF:] * EXP2_SCALE - shift[:, HALF:])
            total = jnp.concatenate(
                [total[:, :HALF], total[:, HALF:] + jnp.sum(e, axis=0, keepdims=True)], axis=1
            )
            e = e.astype(BF16)
            eb[hh, HALF:BLOCK, HALF:] = e
            out2 = nn(vt[0, :, HALF:], e)
            out = jnp.concatenate([out[:, :HALF], out[:, HALF:] + out2], axis=1)
            for j, live in enumerate((live1, live2)):
                sh = jnp.where(live, shift, 1e30)
                for half in range(2):
                    rows = slice(BLOCK * (j + 1) + half * HALF, BLOCK * (j + 1) + (half + 1) * HALF)
                    e = jnp.exp2(sb[rows, :] * EXP2_SCALE - sh)
                    total = total + jnp.sum(e, axis=0, keepdims=True)
                    e = e.astype(BF16)
                    eb[hh, rows, :] = e
                    out = out + nn(vt[j + 1, :, half * HALF : (half + 1) * HALF], e)
            recip = 1.0 / total
            rl[hh] = recip
            out = out * recip
            hrows = pl.ds(pl.multiple_of(hh * HD, HD), HD)
            ot[hrows, :] = out
            ob[:, hcols] = out.T.astype(BF16)
            return 0

        lax.fori_loop(0, GROUP, one_head, 0)

    for g in range(KV):
        if g == 0:
            q_in.wait()
        for k in (1, 2, 3):
            serve_own[g][k - 1].wait_recv()
        forward(g)
        og_chip[g].wait_recv()
        og_pass[g].start()

    def project(block, put):
        def step(i, _):
            n0 = pl.multiple_of(i * 256, 256)
            cols = pl.ds(pl.multiple_of(block * WIDTH + n0, 256), 256)
            put(pl.ds(n0, 256), nn(ob[...], wv[:, cols]))
            return 0

        lax.fori_loop(0, WIDTH // 256, step, 0)

    def to_core(slot):
        def put(cols, val):
            pcs[slot, :, cols] = val.astype(BF16)

        return put

    def to_chip(cols, val):
        pxs[:, cols] = val.astype(BF16)

    def keep(cols, val):
        pown[:, cols] = val

    p_core = [remote(pcs.at[i], pcr.at[i], pcss.at[i], pcrs.at[i], ctx, other_core) for i in range(2)]
    p_chip = remote(pxs, pxr, pxss.at[0], pxrs.at[0], ctx, other_chip)
    project(diagonal, to_core(0))
    p_core[0].start()
    project(other_chip, to_chip)
    p_core[0].wait_recv()
    pxs[...] = (pxs[...].astype(F32) + pcr[0].astype(F32)).astype(BF16)
    p_chip.start()
    project(other_core, to_core(1))
    p_core[1].start()
    project(head, keep)

    for i in range(OG_CUTS):
        og_pass[i].wait_recv()
    grad_block(other_chip, False)
    grad_block(diagonal, False)

    def backward(g, start, stop):
        w_ = win[g]
        if start == 0:
            kt[0] = own[g, 0].T
            kt[1] = w_[col1, 0].T
            kt[2] = w_[col2, 0].T
            acc[g] = jnp.zeros(acc.shape[1:], F32)

        def one_head(r, _):
            hh = g * GROUP + r
            hcols = pl.ds(pl.multiple_of(hh * HD, HD), HD)
            hrows = pl.ds(pl.multiple_of(hh * HD, HD), HD)
            q = qv[:, hcols]
            do32 = dot_[hrows, :] * rl[hh]
            do = do32.astype(BF16)
            rd = jnp.sum(do32 * ot[hrows, :], axis=0, keepdims=True)
            e = eb[hh, 0:HALF, :]
            dp = nn(own[g, 1, :HALF], do)
            dsv = (e.astype(F32) * (dp - rd)).astype(BF16)
            acc[g, 1, 0, :HALF] += nt(e, do)
            acc[g, 0, 0, :HALF] += nn(dsv, q)
            dqt = nn(kt[0, :, :HALF], dsv)
            e = eb[hh, HALF:BLOCK, HALF:]
            dp = nn(own[g, 1, HALF:], do[:, HALF:])
            dsv = (e.astype(F32) * (dp - rd[:, HALF:])).astype(BF16)
            acc[g, 1, 0, HALF:] += nt(e, do[:, HALF:])
            acc[g, 0, 0, HALF:] += nn(dsv, q[HALF:])
            dqt2 = nn(kt[0, :, HALF:], dsv)
            dqt = jnp.concatenate([dqt[:, :HALF], dqt[:, HALF:] + dqt2], axis=1)
            for j, col in enumerate((col1, col2)):
                for half in range(2):
                    part = slice(half * HALF, (half + 1) * HALF)
                    rows = slice(BLOCK * (j + 1) + half * HALF, BLOCK * (j + 1) + (half + 1) * HALF)
                    e = eb[hh, rows, :]
                    dp = nn(w_[col, 1, part], do)
                    dsv = (e.astype(F32) * (dp - rd)).astype(BF16)
                    acc[g, 1, j + 1, part] += nt(e, do)
                    acc[g, 0, j + 1, part] += nn(dsv, q)
                    dqt = dqt + nn(kt[j + 1, :, part], dsv)
            dqv[:, hcols] = (dqt * SCALE).T.astype(BF16)
            return 0

        lax.fori_loop(start, stop, one_head, 0)

    give = [
        [
            remote(
                gs[g].at[lax.rem(y + ROW - k, ROW)], gr[g].at[k - 1], bds.at[g, k - 1], bdr.at[g, k - 1],
                row_start + lax.rem(y + ROW - k, ROW), head,
            )
            for k in (1, 2, 3)
        ]
        for g in range(KV)
    ]
    give_back = [remote(gxs.at[g], gxr.at[g], bxs.at[g], bxr.at[g], preceding, head) for g in range(KV)]

    def send_grads(g):
        for part in range(2):
            factor = SCALE if part == 0 else 1.0
            one = acc[g, part, 1] * factor
            two = acc[g, part, 2] * factor
            for c in range(ROW):
                gs[g][c, part] = (jnp.where(col1 == c, one, 0.0) + jnp.where(col2 == c, two, 0.0)).astype(BF16)
        for k in (1, 3, 2):
            give[g][k - 1].start()

    def sum_grads(g):
        for k in (1, 2, 3):
            give[g][k - 1].wait_recv()
        for part in range(2):
            factor = SCALE if part == 0 else 1.0
            mine = acc[g, part, 0] * factor
            back = gs[g][y, part].astype(F32)
            for k in (1, 2, 3):
                came = gr[g][k - 1, part].astype(F32)
                inside = y + k < ROW
                mine = mine + jnp.where(inside, came, 0.0)
                back = back + jnp.where(inside, 0.0, came)
            acc[g, part, 0] = mine
            gxs[g, part] = back.astype(BF16)
        give_back[g].start()

    outs = []

    def finish_grads(g):
        give_back[g].wait_recv()
        for part in range(2):
            dkv_out[g, part] = (acc[g, part, 0] + gxr[g, part].astype(F32)).astype(BF16)
        for part, ref in ((0, dk_hbm), (1, dv_hbm)):
            cp = pltpu.make_async_copy(dkv_out.at[g, part], ref.at[:, pl.ds(g * HD, HD)], osem.at[2 * g + part])
            cp.start()
            outs.append(cp)

    backward(0, 0, GROUP)
    send_grads(0)
    backward(1, 0, 2)
    sum_grads(0)
    backward(1, 2, GROUP)
    send_grads(1)
    cp = pltpu.make_async_copy(dqv, dq_hbm, osem.at[4])
    cp.start()
    outs.append(cp)
    finish_grads(0)
    p_core[1].wait_recv()
    p_chip.wait_recv()
    pown[...] = pown[...] + pcr[1].astype(F32) + pxr[...].astype(F32)
    pxs_done = p_chip
    pxs_done.wait_send()
    pxs[...] = pown[...].astype(BF16)
    cp = pltpu.make_async_copy(pxs, proj_hbm, osem.at[5])
    cp.start()
    outs.append(cp)
    sum_grads(1)
    finish_grads(1)

    og_core.wait_send()
    for i in range(OG_CUTS):
        og_chip[i].wait_send()
        og_pass[i].wait_send()
    for i in range(2):
        p_core[i].wait_send()
    for g in range(KV):
        cross[g].wait_send()
        give_back[g].wait_send()
        for k in (1, 2, 3):
            serve_own[g][k - 1].wait_send()
            give[g][k - 1].wait_send()
    for cp in outs:
        cp.wait()


def local(queries, keys, values, selected, out_weight, out_grad):
    vm = pltpu.VMEM
    dma = pltpu.SemaphoreType.DMA
    anyspec = pl.BlockSpec(memory_space=pl.ANY)
    return pl.pallas_call(
        kernel,
        out_shape=(
            jax.ShapeDtypeStruct((BLOCK, WIDTH), BF16),
            jax.ShapeDtypeStruct((BLOCK, WIDTH), BF16),
            jax.ShapeDtypeStruct((BLOCK, KV * HD), BF16),
            jax.ShapeDtypeStruct((BLOCK, KV * HD), BF16),
        ),
        in_specs=[pl.BlockSpec(memory_space=pltpu.SMEM)] + [anyspec] * 5,
        out_specs=(anyspec,) * 4,
        scratch_shapes=[
            vm((KV, 2, BLOCK, HD), BF16),
            vm((ROW, 2, BLOCK, HD), BF16),
            vm((ROW, 2, BLOCK, HD), BF16),
            vm((3, HD, BLOCK), BF16),
            vm((3, HD, BLOCK), BF16),
            vm((BLOCK, WIDTH), BF16),
            vm((WIDTH, 4 * WIDTH), BF16),
            vm((4, BLOCK, WIDTH), BF16),
            vm((WIDTH, BLOCK), F32),
            vm((WIDTH, BLOCK), F32),
            vm((BLOCK, WIDTH), BF16),
            vm((KV * GROUP, 1, BLOCK), F32),
            vm((KV * GROUP, 3 * BLOCK, BLOCK), BF16),
            vm((3 * BLOCK, BLOCK), F32),
            vm((KV, 2, 3, BLOCK, HD), F32),
            vm((ROW, 2, BLOCK, HD), BF16),
            vm((ROW, 2, BLOCK, HD), BF16),
            vm((3, 2, BLOCK, HD), BF16),
            vm((3, 2, BLOCK, HD), BF16),
            vm((KV, 2, BLOCK, HD), BF16),
            vm((KV, 2, BLOCK, HD), BF16),
            vm((2, BLOCK, WIDTH), BF16),
            vm((2, BLOCK, WIDTH), BF16),
            vm((BLOCK, WIDTH), BF16),
            vm((BLOCK, WIDTH), BF16),
            vm((BLOCK, WIDTH), F32),
            vm((BLOCK, WIDTH), BF16),
            vm((KV, 2, BLOCK, HD), BF16),
            dma((7,)), dma((6,)),
            dma((KV,)), dma((KV,)), dma((KV, 3)), dma((KV, 3)),
            dma((1,)), dma((1,)), dma((OG_CUTS,)), dma((OG_CUTS,)), dma((OG_CUTS,)), dma((OG_CUTS,)),
            dma((2,)), dma((2,)), dma((1,)), dma((1,)),
            dma((KV, 3)), dma((KV, 3)), dma((KV,)), dma((KV,)),
        ],
        compiler_params=pltpu.CompilerParams(
            collective_id=0, has_side_effects=True, vmem_limit_bytes=63 * 1024 * 1024
        ),
        cost_estimate=pl.CostEstimate(flops=18 * 10**9, bytes_accessed=16 * 2**20, transcendentals=6 * 10**6),
        name="layer",
    )(selected, queries, keys, values, out_weight, out_grad)


def solution(mesh):
    placed = (
        P("ctx", "head"),
        P("ctx", "head"),
        P("ctx", "head"),
        P("ctx", None),
        P("head", None),
        P("ctx", "head"),
    )
    return jax.shard_map(
        local,
        mesh=mesh,
        in_specs=placed,
        out_specs=(P("ctx", "head"), P("ctx", "head"), P("ctx", "head"), P("ctx", "head")),
        check_vma=False,
    )
```

profile of v0, /device:TPU:1, one launch (start us, length us, event | category | flops | bytes accessed | tf_op | source)
XLA Modules:
  0.0 115.5 jit_solution(4636175649909259730)
XLA Ops:
  0.6 107.0 %layer.1 = (bf16[512,1024]{1,0:T(8,128)(2,1)}, bf16[512,1024]{1,0:T(8,128)(2,1)}, bf16[512,256]{1,0:T(8,128)(2,1)}, bf16[512,256]{1,0:T(8,128)(2,1)}) custom-call(s32[1,3]{1,0:T(1,128)} %sel.1, bf16[512,1024]{1,0:T(8,128)(2,1)} %q_hbm.1, bf16[512,256]{1,0:T(8,128)(2,1)} %k_hbm.1, bf16[512,256]{1,0:T(8,128)(2,1)} %v_hbm.1, bf16[1024,4096]{1,0:T(8,128)(2,1)} %w_hbm.1, ...), custom_call_target="tpu_custom_call" | custom-call | flops 17999998976 | bytes 16777216 | tf_op jit(solution)/shard_map/layer/pallas_call | solution.py:396
  107.7 2.3 %copy.14 = bf16[512,1024]{1,0:T(8,128)(2,1)} copy(bf16[512,1024]{1,0:T(8,128)(2,1)} %get-tuple-element.8) | data formatting | bytes 2097152
  109.9 2.3 %copy.15 = bf16[512,1024]{1,0:T(8,128)(2,1)} copy(bf16[512,1024]{1,0:T(8,128)(2,1)} %get-tuple-element.9) | data formatting | bytes 2097152
  112.2 1.7 %copy.16 = bf16[512,256]{1,0:T(8,128)(2,1)} copy(bf16[512,256]{1,0:T(8,128)(2,1)} %get-tuple-element.10) | data formatting | bytes 524288
  113.9 1.7 %copy.17 = bf16[512,256]{1,0:T(8,128)(2,1)} copy(bf16[512,256]{1,0:T(8,128)(2,1)} %get-tuple-element.11) | data formatting | bytes 524288
where the time goes:
time: 116 us
  Pallas kernels  107 us (92%)
  local copies, waits for them, and re-layouts  7.86 us (7%)
    pallas_call x1, Pallas kernels, local(): pl.pallas_call(kernel, out_shape=(jax.ShapeDtypeStruct((BLOCK, WIDTH), BF...  107 us
    unnamed x4, local copies, waits for them, and re-layouts  7.86 us

commit v1 on v0

--- a/solution.py
+++ b/solution.py
@@ -22,6 +22,9 @@
 F32 = jnp.float32
 OG_CUTS = 2
 OG_ROWS = BLOCK // OG_CUTS
+CUTS = 2
+CUT = WIDTH // CUTS
+MOVES = [(n, i * 128, 128) for n in (0, 1) for i in range(4)] + [(n, i * 256, 256) for n in (2, 3) for i in range(2)]
 
 
 def nn(a, b):
@@ -36,7 +39,7 @@
     sel, q_hbm, k_hbm, v_hbm, w_hbm, og_hbm,
     proj_hbm, dq_hbm, dk_hbm, dv_hbm,
     own, win0, win1, vt, kt, qv, wv, ogb, dot_, ot, ob, rl, eb, sb, acc,
-    gs0, gs1, gr0, gr1, gxs, gxr, pcs, pcr, pxs, pxr, pown, dqv, dkv_out,
+    gs0, gs1, gr0, gr1, gxs, gxr, pcs, pcr, pxs, pxr, pown, dqv, dkv_out, dob, rdb,
     lsem, osem, xs, xr, ds_, dr, ocs, ocr, oxs, oxr, ofs, ofr, pcss, pcrs, pxss, pxrs, bds, bdr, bxs, bxr,
 ):
     win = (win0, win1)
@@ -103,8 +106,9 @@
         kv_in[g][0].wait()
         kv_in[g][1].wait()
         cross[g].start()
-        for k in (1, 3, 2):
-            pl.when(y + k < ROW)(serve_own[g][k - 1].start)
+        if g == 0:
+            for k in (1, 3, 2):
+                pl.when(y + k < ROW)(serve_own[g][k - 1].start)
 
     og_in.wait()
     og_core = remote(ogb.at[head], ogb.at[head], ocs.at[0], ocr.at[0], ctx, other_core)
@@ -138,10 +142,14 @@
         cross[g].wait_recv()
         for k in (3, 1, 2):
             pl.when(y + k >= ROW)(serve_prev[g][k - 1].start)
-        og_chip[g].start()
         if g == 0:
+            for k in (1, 3, 2):
+                pl.when(y + k < ROW)(serve_own[1][k - 1].start)
             og_core.wait_recv()
             grad_block(other_core, False)
+        else:
+            for i in range(OG_CUTS):
+                og_chip[i].start()
 
     sel1 = sel[0, 1]
     sel2 = sel[0, 2]
@@ -217,190 +225,243 @@
         for k in (1, 2, 3):
             serve_own[g][k - 1].wait_recv()
         forward(g)
-        og_chip[g].wait_recv()
-        og_pass[g].start()
-
-    def project(block, put):
+
+    def project(block, cut, put):
         def step(i, _):
             n0 = pl.multiple_of(i * 256, 256)
-            cols = pl.ds(pl.multiple_of(block * WIDTH + n0, 256), 256)
+            cols = pl.ds(pl.multiple_of(block * WIDTH + cut * CUT + n0, 256), 256)
             put(pl.ds(n0, 256), nn(ob[...], wv[:, cols]))
             return 0
 
-        lax.fori_loop(0, WIDTH // 256, step, 0)
-
-    def to_core(slot):
+        lax.fori_loop(0, CUT // 256, step, 0)
+
+    def to_core(slot, cut):
         def put(cols, val):
-            pcs[slot, :, cols] = val.astype(BF16)
+            pcs[slot, cut, :, cols] = val.astype(BF16)
 
         return put
 
-    def to_chip(cols, val):
-        pxs[:, cols] = val.astype(BF16)
-
-    def keep(cols, val):
-        pown[:, cols] = val
-
-    p_core = [remote(pcs.at[i], pcr.at[i], pcss.at[i], pcrs.at[i], ctx, other_core) for i in range(2)]
-    p_chip = remote(pxs, pxr, pxss.at[0], pxrs.at[0], ctx, other_chip)
-    project(diagonal, to_core(0))
-    p_core[0].start()
-    project(other_chip, to_chip)
-    p_core[0].wait_recv()
-    pxs[...] = (pxs[...].astype(F32) + pcr[0].astype(F32)).astype(BF16)
-    p_chip.start()
-    project(other_core, to_core(1))
-    p_core[1].start()
-    project(head, keep)
-
+    def to_chip(cut):
+        def put(cols, val):
+            pxs[cut, :, cols] = (val + pcr[0, cut, :, cols].astype(F32)).astype(BF16)
+
+        return put
+
+    def keep(cut):
+        def put(cols, val):
+            pown[cut, :, cols] = val
+
+        return put
+
+    p_core = [
+        [remote(pcs.at[i, j], pcr.at[i, j], pcss.at[i, j], pcrs.at[i, j], ctx, other_core) for j in range(CUTS)]
+        for i in range(2)
+    ]
+    p_chip = [remote(pxs.at[j], pxr.at[j], pxss.at[j], pxrs.at[j], ctx, other_chip) for j in range(CUTS)]
+    project(diagonal, 0, to_core(0, 0))
+    p_core[0][0].start()
+    project(diagonal, 1, to_core(0, 1))
+    p_core[0][1].start()
+    for j in range(CUTS):
+        p_core[0][j].wait_recv()
+        project(other_chip, j, to_chip(j))
+        p_chip[j].start()
+        if j == 0:
+            for i in range(OG_CUTS):
+                og_chip[i].wait_recv()
+                og_pass[i].start()
+    grad_block(other_chip, False)
     for i in range(OG_CUTS):
         og_pass[i].wait_recv()
-    grad_block(other_chip, False)
     grad_block(diagonal, False)
 
-    def backward(g, start, stop):
+    def back_tile(g, slot, w_, col, part, hh, q, do, rd, span):
+        keys_at = slice(part * HALF, (part + 1) * HALF)
+        e = eb[hh, slot * BLOCK + part * HALF : slot * BLOCK + (part + 1) * HALF, span]
+        v = own[g, 1, keys_at] if slot == 0 else w_[col, 1, keys_at]
+        dp = nn(v, do)
+        dsv = (e.astype(F32) * (dp - rd)).astype(BF16)
+        acc[g, 1, slot, keys_at] += nt(e, do)
+        acc[g, 0, slot, keys_at] += nn(dsv, q)
+        return nn(kt[slot, :, keys_at], dsv)
+
+    def backward_far(g):
         w_ = win[g]
-        if start == 0:
-            kt[0] = own[g, 0].T
-            kt[1] = w_[col1, 0].T
-            kt[2] = w_[col2, 0].T
-            acc[g] = jnp.zeros(acc.shape[1:], F32)
+        kt[1] = w_[col1, 0].T
+        kt[2] = w_[col2, 0].T
+        acc[g] = jnp.zeros(acc.shape[1:], F32)
 
         def one_head(r, _):
             hh = g * GROUP + r
             hcols = pl.ds(pl.multiple_of(hh * HD, HD), HD)
-            hrows = pl.ds(pl.multiple_of(hh * HD, HD), HD)
             q = qv[:, hcols]
-            do32 = dot_[hrows, :] * rl[hh]
+            do32 = dot_[hcols, :] * rl[hh]
             do = do32.astype(BF16)
-            rd = jnp.sum(do32 * ot[hrows, :], axis=0, keepdims=True)
-            e = eb[hh, 0:HALF, :]
-            dp = nn(own[g, 1, :HALF], do)
-            dsv = (e.astype(F32) * (dp - rd)).astype(BF16)
-            acc[g, 1, 0, :HALF] += nt(e, do)
-            acc[g, 0, 0, :HALF] += nn(dsv, q)
-            dqt = nn(kt[0, :, :HALF], dsv)
-            e = eb[hh, HALF:BLOCK, HALF:]
-            dp = nn(own[g, 1, HALF:], do[:, HALF:])
-            dsv = (e.astype(F32) * (dp - rd[:, HALF:])).astype(BF16)
-            acc[g, 1, 0, HALF:] += nt(e, do[:, HALF:])
-            acc[g, 0, 0, HALF:] += nn(dsv, q[HALF:])
-            dqt2 = nn(kt[0, :, HALF:], dsv)
-            dqt = jnp.concatenate([dqt[:, :HALF], dqt[:, HALF:] + dqt2], axis=1)
-            for j, col in enumerate((col1, col2)):
-                for half in range(2):
-                    part = slice(half * HALF, (half + 1) * HALF)
-                    rows = slice(BLOCK * (j + 1) + half * HALF, BLOCK * (j + 1) + (half + 1) * HALF)
-                    e = eb[hh, rows, :]
-                    dp = nn(w_[col, 1, part], do)
-                    dsv = (e.astype(F32) * (dp - rd)).astype(BF16)
-                    acc[g, 1, j + 1, part] += nt(e, do)
-                    acc[g, 0, j + 1, part] += nn(dsv, q)
-                    dqt = dqt + nn(kt[j + 1, :, part], dsv)
+            rd = jnp.sum(do32 * ot[hcols, :], axis=0, keepdims=True)
+            dob[hcols, :] = do
+            rdb[hh] = rd
+            dqt = jnp.zeros((HD, BLOCK), F32)
+            for slot, col in ((1, col1), (2, col2)):
+                for part in range(2):
+                    dqt = dqt + back_tile(g, slot, w_, col, part, hh, q, do, rd, slice(None))
+            dot_[hcols, :] = dqt
+            return 0
+
+        lax.fori_loop(0, GROUP, one_head, 0)
+
+    def backward_near(g):
+        kt[0] = own[g, 0].T
+
+        def one_head(r, _):
+            hh = g * GROUP + r
+            hcols = pl.ds(pl.multiple_of(hh * HD, HD), HD)
+            q = qv[:, hcols]
+            do = dob[hcols, :]
+            rd = rdb[hh]
+            dqt = dot_[hcols, :] + back_tile(g, 0, None, None, 0, hh, q, do, rd, slice(None))
+            late = back_tile(g, 0, None, None, 1, hh, q[HALF:], do[:, HALF:], rd[:, HALF:], slice(HALF, BLOCK))
+            dqt = jnp.concatenate([dqt[:, :HALF], dqt[:, HALF:] + late], axis=1)
             dqv[:, hcols] = (dqt * SCALE).T.astype(BF16)
             return 0
 
-        lax.fori_loop(start, stop, one_head, 0)
+        lax.fori_loop(0, GROUP, one_head, 0)
 
     give = [
         [
-            remote(
-                gs[g].at[lax.rem(y + ROW - k, ROW)], gr[g].at[k - 1], bds.at[g, k - 1], bdr.at[g, k - 1],
-                row_start + lax.rem(y + ROW - k, ROW), head,
-            )
-            for k in (1, 2, 3)
+            [
+                remote(
+                    gs[g].at[lax.rem(y + ROW - k, ROW), part], gr[g].at[k - 1, part],
+                    bds.at[g, part, k - 1], bdr.at[g, part, k - 1],
+                    row_start + lax.rem(y + ROW - k, ROW), head,
+                )
+                for k in (1, 2, 3)
+            ]
+            for part in range(2)
         ]
         for g in range(KV)
     ]
-    give_back = [remote(gxs.at[g], gxr.at[g], bxs.at[g], bxr.at[g], preceding, head) for g in range(KV)]
-
-    def send_grads(g):
-        for part in range(2):
-            factor = SCALE if part == 0 else 1.0
-            one = acc[g, part, 1] * factor
-            two = acc[g, part, 2] * factor
-            for c in range(ROW):
-                gs[g][c, part] = (jnp.where(col1 == c, one, 0.0) + jnp.where(col2 == c, two, 0.0)).astype(BF16)
+    give_back = [
+        [
+            remote(gxs.at[g, part], gxr.at[g, part], bxs.at[g, part], bxr.at[g, part], preceding, head)
+            for part in range(2)
+        ]
+        for g in range(KV)
+    ]
+    factors = (SCALE, 1.0)
+
+    def send_grads(g, part):
+        one = acc[g, part, 1] * factors[part]
+        two = acc[g, part, 2] * factors[part]
+        for c in range(ROW):
+            gs[g][c, part] = (jnp.where(col1 == c, one, 0.0) + jnp.where(col2 == c, two, 0.0)).astype(BF16)
         for k in (1, 3, 2):
-            give[g][k - 1].start()
-
-    def sum_grads(g):
+            give[g][part][k - 1].start()
+
+    def sum_grads(g, part):
         for k in (1, 2, 3):
-            give[g][k - 1].wait_recv()
-        for part in range(2):
-            factor = SCALE if part == 0 else 1.0
-            mine = acc[g, part, 0] * factor
-            back = gs[g][y, part].astype(F32)
-            for k in (1, 2, 3):
-                came = gr[g][k - 1, part].astype(F32)
-                inside = y + k < ROW
-                mine = mine + jnp.where(inside, came, 0.0)
-                back = back + jnp.where(inside, 0.0, came)
-            acc[g, part, 0] = mine
-            gxs[g, part] = back.astype(BF16)
-        give_back[g].start()
+            give[g][part][k - 1].wait_recv()
+        mine = acc[g, part, 0] * factors[part]
+        back = gs[g][y, part].astype(F32)
+        for k in (1, 2, 3):
+            came = gr[g][k - 1, part].astype(F32)
+            inside = y + k < ROW
+            mine = mine + jnp.where(inside, came, 0.0)
+            back = back + jnp.where(inside, 0.0, came)
+        gxs[g, part] = back.astype(BF16)
+        give_back[g][part].start()
+        acc[g, part, 0] = mine
 
     outs = []
 
-    def finish_grads(g):
-        give_back[g].wait_recv()
-        for part in range(2):
-            dkv_out[g, part] = (acc[g, part, 0] + gxr[g, part].astype(F32)).astype(BF16)
-        for part, ref in ((0, dk_hbm), (1, dv_hbm)):
-            cp = pltpu.make_async_copy(dkv_out.at[g, part], ref.at[:, pl.ds(g * HD, HD)], osem.at[2 * g + part])
-            cp.start()
-            outs.append(cp)
-
-    backward(0, 0, GROUP)
-    send_grads(0)
-    backward(1, 0, 2)
-    sum_grads(0)
-    backward(1, 2, GROUP)
-    send_grads(1)
+    def finish_grads(g, part):
+        give_back[g][part].wait_recv()
+        dkv_out[g, part] = (acc[g, part, 0] + gxr[g, part].astype(F32)).astype(BF16)
+        ref = (dk_hbm, dv_hbm)[part]
+        cp = pltpu.make_async_copy(dkv_out.at[g, part], ref.at[:, pl.ds(g * HD, HD)], osem.at[2 * g + part])
+        cp.start()
+        outs.append(cp)
+
+    for g in range(KV):
+        backward_far(g)
+        for part in (1, 0):
+            send_grads(g, part)
+    for g in range(KV):
+        backward_near(g)
     cp = pltpu.make_async_copy(dqv, dq_hbm, osem.at[4])
     cp.start()
     outs.append(cp)
-    finish_grads(0)
-    p_core[1].wait_recv()
-    p_chip.wait_recv()
-    pown[...] = pown[...] + pcr[1].astype(F32) + pxr[...].astype(F32)
-    pxs_done = p_chip
-    pxs_done.wait_send()
-    pxs[...] = pown[...].astype(BF16)
-    cp = pltpu.make_async_copy(pxs, proj_hbm, osem.at[5])
-    cp.start()
-    outs.append(cp)
-    sum_grads(1)
-    finish_grads(1)
+    for j in range(CUTS):
+        project(other_core, j, to_core(1, j))
+        p_core[1][j].start()
+    for part in (1, 0):
+        sum_grads(0, part)
+    for j in range(CUTS):
+        project(head, j, keep(j))
+    sum_grads(1, 1)
+    for j in range(CUTS):
+        p_core[1][j].wait_recv()
+        p_chip[j].wait()
+        pxs[j] = (pown[j] + pcr[1, j].astype(F32) + pxr[j].astype(F32)).astype(BF16)
+        cp = pltpu.make_async_copy(pxs.at[j], proj_hbm.at[:, pl.ds(j * CUT, CUT)], osem.at[5 + j])
+        cp.start()
+        outs.append(cp)
+    sum_grads(1, 0)
+    for g in range(KV):
+        for part in (1, 0):
+            finish_grads(g, part)
 
     og_core.wait_send()
     for i in range(OG_CUTS):
         og_chip[i].wait_send()
         og_pass[i].wait_send()
     for i in range(2):
-        p_core[i].wait_send()
+        for j in range(CUTS):
+            p_core[i][j].wait_send()
     for g in range(KV):
         cross[g].wait_send()
-        give_back[g].wait_send()
         for k in (1, 2, 3):
             serve_own[g][k - 1].wait_send()
-            give[g][k - 1].wait_send()
+        for part in range(2):
+            give_back[g][part].wait_send()
+            for k in (1, 2, 3):
+                give[g][part][k - 1].wait_send()
     for cp in outs:
         cp.wait()
+
+
+def mover(*refs):
+    ins, outs, held, sems = refs[:4], refs[4:8], refs[8:12], refs[12]
+    copies = []
+    for i, (n, first, rows) in enumerate(MOVES):
+        at = pl.ds(first, rows)
+        copies.append(
+            (
+                pltpu.make_async_copy(ins[n].at[at], held[n].at[at], sems.at[0, i]),
+                pltpu.make_async_copy(held[n].at[at], outs[n].at[at], sems.at[1, i]),
+            )
+        )
+    for come, _ in copies:
+        come.start()
+    for come, go in copies:
+        come.wait()
+        go.start()
+    for _, go in copies:
+        go.wait()
 
 
 def local(queries, keys, values, selected, out_weight, out_grad):
     vm = pltpu.VMEM
     dma = pltpu.SemaphoreType.DMA
     anyspec = pl.BlockSpec(memory_space=pl.ANY)
-    return pl.pallas_call(
+    shapes = (
+        jax.ShapeDtypeStruct((BLOCK, WIDTH), BF16),
+        jax.ShapeDtypeStruct((BLOCK, WIDTH), BF16),
+        jax.ShapeDtypeStruct((BLOCK, KV * HD), BF16),
+        jax.ShapeDtypeStruct((BLOCK, KV * HD), BF16),
+    )
+    results = pl.pallas_call(
         kernel,
-        out_shape=(
-            jax.ShapeDtypeStruct((BLOCK, WIDTH), BF16),
-            jax.ShapeDtypeStruct((BLOCK, WIDTH), BF16),
-            jax.ShapeDtypeStruct((BLOCK, KV * HD), BF16),
-            jax.ShapeDtypeStruct((BLOCK, KV * HD), BF16),
-        ),
+        out_shape=shapes,
         in_specs=[pl.BlockSpec(memory_space=pltpu.SMEM)] + [anyspec] * 5,
         out_specs=(anyspec,) * 4,
         scratch_shapes=[
@@ -425,18 +486,20 @@
             vm((3, 2, BLOCK, HD), BF16),
             vm((KV, 2, BLOCK, HD), BF16),
             vm((KV, 2, BLOCK, HD), BF16),
-            vm((2, BLOCK, WIDTH), BF16),
-            vm((2, BLOCK, WIDTH), BF16),
-            vm((BLOCK, WIDTH), BF16),
-            vm((BLOCK, WIDTH), BF16),
-            vm((BLOCK, WIDTH), F32),
+            vm((2, CUTS, BLOCK, CUT), BF16),
+            vm((2, CUTS, BLOCK, CUT), BF16),
+            vm((CUTS, BLOCK, CUT), BF16),
+            vm((CUTS, BLOCK, CUT), BF16),
+            vm((CUTS, BLOCK, CUT), F32),
             vm((BLOCK, WIDTH), BF16),
             vm((KV, 2, BLOCK, HD), BF16),
-            dma((7,)), dma((6,)),
+            vm((WIDTH, BLOCK), BF16),
+            vm((KV * GROUP, 1, BLOCK), F32),
+            dma((7,)), dma((5 + CUTS,)),
             dma((KV,)), dma((KV,)), dma((KV, 3)), dma((KV, 3)),
             dma((1,)), dma((1,)), dma((OG_CUTS,)), dma((OG_CUTS,)), dma((OG_CUTS,)), dma((OG_CUTS,)),
-            dma((2,)), dma((2,)), dma((1,)), dma((1,)),
-            dma((KV, 3)), dma((KV, 3)), dma((KV,)), dma((KV,)),
+            dma((2, CUTS)), dma((2, CUTS)), dma((CUTS,)), dma((CUTS,)),
+            dma((KV, 2, 3)), dma((KV, 2, 3)), dma((KV, 2)), dma((KV, 2)),
         ],
         compiler_params=pltpu.CompilerParams(
             collective_id=0, has_side_effects=True, vmem_limit_bytes=63 * 1024 * 1024
@@ -444,6 +507,15 @@
         cost_estimate=pl.CostEstimate(flops=18 * 10**9, bytes_accessed=16 * 2**20, transcendentals=6 * 10**6),
         name="layer",
     )(selected, queries, keys, values, out_weight, out_grad)
+    return pl.pallas_call(
+        mover,
+        out_shape=shapes,
+        in_specs=[anyspec] * 4,
+        out_specs=(anyspec,) * 4,
+        scratch_shapes=[vm(x.shape, x.dtype) for x in shapes] + [dma((2, len(MOVES)))],
+        compiler_params=pltpu.CompilerParams(vmem_limit_bytes=60 * 1024 * 1024),
+        name="move",
+    )(*results)
 
 
 def solution(mesh):

time: 116 us -> 93.8 us (0.81)
  Pallas kernels: 107 us -> 91.7 us
  local copies, waits for them, and re-layouts: 7.86 us -> 0 us
    pallas_call x1 -> x2, Pallas kernels: 107 us -> 91.7 us  [the longest x1 89 us: local(): pl.pallas_call(kernel, out_shape=shapes, in_specs=[pl.BlockSpec(memory_sp...]
    unnamed x4 -> x0, local copies, waits for them, and re-layouts: 7.86 us -> none
where the time goes in v1:
time: 93.8 us; the launch traced here: 92.3 us
  Pallas kernels  91.7 us (98%)
    pallas_call x1, Pallas kernels, local(): pl.pallas_call(kernel, out_shape=shapes, in_specs=[pl.BlockSpec(memory_sp...  89 us
    pallas_call x1, Pallas kernels, local(): pl.pallas_call(mover, out_shape=shapes, in_specs=[anyspec] * 4, out_specs...  2.63 us

profile of v1, /device:TPU:1, one launch (start us, length us, event | category | flops | bytes accessed | tf_op | source)
XLA Modules:
  0.0 92.3 jit_solution(13641414970049589678)
XLA Ops:
  0.6 89.0 %layer.1 = (bf16[512,1024]{1,0:T(8,128)(2,1)}, bf16[512,1024]{1,0:T(8,128)(2,1)}, bf16[512,256]{1,0:T(8,128)(2,1)}, bf16[512,256]{1,0:T(8,128)(2,1)}) custom-call(s32[1,3]{1,0:T(1,128)} %sel.1, bf16[512,1024]{1,0:T(8,128)(2,1)} %q_hbm.1, bf16[512,256]{1,0:T(8,128)(2,1)} %k_hbm.1, bf16[512,256]{1,0:T(8,128)(2,1)} %v_hbm.1, bf16[1024,4096]{1,0:T(8,128)(2,1)} %w_hbm.1, ...), custom_call_target="tpu_custom_call" | custom-call | flops 17999998976 | bytes 16777216 | tf_op jit(solution)/shard_map/layer/pallas_call | solution.py:462
  89.7 2.6 %move.1 = (bf16[512,1024]{1,0:T(8,128)(2,1)}, bf16[512,1024]{1,0:T(8,128)(2,1)}, bf16[512,256]{1,0:T(8,128)(2,1)}, bf16[512,256]{1,0:T(8,128)(2,1)}) custom-call(bf16[512,1024]{1,0:T(8,128)(2,1)} %get-tuple-element.8.refs_0_, bf16[512,1024]{1,0:T(8,128)(2,1)} %get-tuple-element.9.refs_1_, bf16[512,256]{1,0:T(8,128)(2,1)} %get-tuple-element.10.refs_2_, ...), custom_call_target="tpu_custom_call" | custom-call | tf_op jit(solution)/shard_map/move/pallas_call | solution.py:510

commit v2 on v1

--- a/solution.py
+++ b/solution.py
@@ -39,7 +39,7 @@
     sel, q_hbm, k_hbm, v_hbm, w_hbm, og_hbm,
     proj_hbm, dq_hbm, dk_hbm, dv_hbm,
     own, win0, win1, vt, kt, qv, wv, ogb, dot_, ot, ob, rl, eb, sb, acc,
-    gs0, gs1, gr0, gr1, gxs, gxr, pcs, pcr, pxs, pxr, pown, dqv, dkv_out, dob, rdb,
+    gs0, gs1, gr0, gr1, gxs, gxr, pcs, pcr, pxs, pxr, pown, dqv, dkv_out, dob, rdb, top0, total0, fades,
     lsem, osem, xs, xr, ds_, dr, ocs, ocr, oxs, oxr, ofs, ofr, pcss, pcrs, pxss, pxrs, bds, bdr, bxs, bxr,
 ):
     win = (win0, win1)
@@ -145,11 +145,11 @@
         if g == 0:
             for k in (1, 3, 2):
                 pl.when(y + k < ROW)(serve_own[1][k - 1].start)
-            og_core.wait_recv()
-            grad_block(other_core, False)
         else:
             for i in range(OG_CUTS):
                 og_chip[i].start()
+    og_core.wait_recv()
+    grad_block(other_core, False)
 
     sel1 = sel[0, 1]
     sel2 = sel[0, 2]
@@ -161,11 +161,8 @@
     key_pos = lax.broadcasted_iota(jnp.int32, (HALF, BLOCK), 0)
     query_pos = lax.broadcasted_iota(jnp.int32, (HALF, BLOCK), 1)
 
-    def forward(g):
-        w_ = win[g]
+    def forward_near(g):
         vt[0] = own[g, 1].T
-        vt[1] = w_[col1, 1].T
-        vt[2] = w_[col2, 1].T
 
         def one_head(r, _):
             hh = g * GROUP + r
@@ -173,58 +170,78 @@
             q = qv[:, hcols]
             s = nt(own[g, 0, :HALF], q)
             s = jnp.where(key_pos <= query_pos, s, -1e30)
-            sb[0:HALF, :] = s
+            late = nt(own[g, 0, HALF:], q[HALF:])
+            late = jnp.where((key_pos <= query_pos)[:, :HALF], late, -1e30)
             top = jnp.max(s, axis=0, keepdims=True)
-            s = nt(own[g, 0, HALF:], q[HALF:])
-            s = jnp.where((key_pos <= query_pos)[:, :HALF], s, -1e30)
-            sb[HALF:BLOCK, HALF:] = s
             top = jnp.concatenate(
-                [top[:, :HALF], jnp.maximum(top[:, HALF:], jnp.max(s, axis=0, keepdims=True))], axis=1
+                [top[:, :HALF], jnp.maximum(top[:, HALF:], jnp.max(late, axis=0, keepdims=True))], axis=1
             )
+            shift = top * EXP2_SCALE
+            e = jnp.exp2(s * EXP2_SCALE - shift)
+            e2 = jnp.exp2(late * EXP2_SCALE - shift[:, HALF:])
+            total = jnp.sum(e, axis=0, keepdims=True)
+            total = jnp.concatenate(
+                [total[:, :HALF], total[:, HALF:] + jnp.sum(e2, axis=0, keepdims=True)], axis=1
+            )
+            e = e.astype(BF16)
+            e2 = e2.astype(BF16)
+            eb[hh, 0:HALF, :] = e
+            eb[hh, HALF:BLOCK, HALF:] = e2
+            out = nn(vt[0, :, :HALF], e)
+            out2 = nn(vt[0, :, HALF:], e2)
+            ot[hcols, :] = jnp.concatenate([out[:, :HALF], out[:, HALF:] + out2], axis=1)
+            top0[hh] = top
+            total0[hh] = total
+            return 0
+
+        lax.fori_loop(0, GROUP, one_head, 0)
+
+    def forward_far(g):
+        w_ = win[g]
+        vt[1] = w_[col1, 1].T
+        vt[2] = w_[col2, 1].T
+
+        def one_head(r, _):
+            hh = g * GROUP + r
+            hcols = pl.ds(pl.multiple_of(hh * HD, HD), HD)
+            q = qv[:, hcols]
+            first_top = top0[hh]
+            top = first_top
             for j, (col, live) in enumerate(((col1, live1), (col2, live2))):
                 for half in range(2):
                     s = nt(w_[col, 0, half * HALF : (half + 1) * HALF], q)
-                    sb[BLOCK * (j + 1) + half * HALF : BLOCK * (j + 1) + (half + 1) * HALF, :] = s
+                    sb[BLOCK * j + half * HALF : BLOCK * j + (half + 1) * HALF, :] = s
                     top = jnp.maximum(top, jnp.where(live, jnp.max(s, axis=0, keepdims=True), -1e30))
             shift = top * EXP2_SCALE
-            e = jnp.exp2(sb[0:HALF, :] * EXP2_SCALE - shift)
-            total = jnp.sum(e, axis=0, keepdims=True)
-            e = e.astype(BF16)
-            eb[hh, 0:HALF, :] = e
-            out = nn(vt[0, :, :HALF], e)
-            e = jnp.exp2(sb[HALF:BLOCK, HALF:] * EXP2_SCALE - shift[:, HALF:])
-            total = jnp.concatenate(
-                [total[:, :HALF], total[:, HALF:] + jnp.sum(e, axis=0, keepdims=True)], axis=1
-            )
-            e = e.astype(BF16)
-            eb[hh, HALF:BLOCK, HALF:] = e
-            out2 = nn(vt[0, :, HALF:], e)
-            out = jnp.concatenate([out[:, :HALF], out[:, HALF:] + out2], axis=1)
+            fade = jnp.exp2(first_top * EXP2_SCALE - shift)
+            total = total0[hh] * fade
+            out = ot[hcols, :] * fade
             for j, live in enumerate((live1, live2)):
                 sh = jnp.where(live, shift, 1e30)
                 for half in range(2):
-                    rows = slice(BLOCK * (j + 1) + half * HALF, BLOCK * (j + 1) + (half + 1) * HALF)
-                    e = jnp.exp2(sb[rows, :] * EXP2_SCALE - sh)
+                    at = BLOCK * j + half * HALF
+                    e = jnp.exp2(sb[at : at + HALF, :] * EXP2_SCALE - sh)
                     total = total + jnp.sum(e, axis=0, keepdims=True)
                     e = e.astype(BF16)
-                    eb[hh, rows, :] = e
+                    eb[hh, BLOCK + at : BLOCK + at + HALF, :] = e
                     out = out + nn(vt[j + 1, :, half * HALF : (half + 1) * HALF], e)
             recip = 1.0 / total
             rl[hh] = recip
+            fades[hh] = fade
             out = out * recip
-            hrows = pl.ds(pl.multiple_of(hh * HD, HD), HD)
-            ot[hrows, :] = out
+            ot[hcols, :] = out
             ob[:, hcols] = out.T.astype(BF16)
             return 0
 
         lax.fori_loop(0, GROUP, one_head, 0)
 
-    for g in range(KV):
-        if g == 0:
-            q_in.wait()
+    q_in.wait()
+    for g in range(KV):
+        forward_near(g)
+    for g in range(KV):
         for k in (1, 2, 3):
             serve_own[g][k - 1].wait_recv()
-        forward(g)
+        forward_far(g)
 
     def project(block, cut, put):
         def step(i, _):
@@ -281,25 +298,33 @@
         v = own[g, 1, keys_at] if slot == 0 else w_[col, 1, keys_at]
         dp = nn(v, do)
         dsv = (e.astype(F32) * (dp - rd)).astype(BF16)
-        acc[g, 1, slot, keys_at] += nt(e, do)
         acc[g, 0, slot, keys_at] += nn(dsv, q)
         return nn(kt[slot, :, keys_at], dsv)
+
+    def value_far(g):
+        for r in range(GROUP):
+            hh = g * GROUP + r
+            hcols = slice(hh * HD, (hh + 1) * HD)
+            do32 = dot_[hcols, :] * rl[hh]
+            do = do32.astype(BF16)
+            rdb[hh] = jnp.sum(do32 * ot[hcols, :], axis=0, keepdims=True)
+            dob[hcols, :] = do
+            for slot in (1, 2):
+                part = nt(eb[hh, slot * BLOCK : (slot + 1) * BLOCK, :], do)
+                acc[g, 1, slot] = part if r == 0 else acc[g, 1, slot] + part
 
     def backward_far(g):
         w_ = win[g]
         kt[1] = w_[col1, 0].T
         kt[2] = w_[col2, 0].T
-        acc[g] = jnp.zeros(acc.shape[1:], F32)
+        acc[g, 0] = jnp.zeros(acc.shape[2:], F32)
 
         def one_head(r, _):
             hh = g * GROUP + r
             hcols = pl.ds(pl.multiple_of(hh * HD, HD), HD)
             q = qv[:, hcols]
-            do32 = dot_[hcols, :] * rl[hh]
-            do = do32.astype(BF16)
-            rd = jnp.sum(do32 * ot[hcols, :], axis=0, keepdims=True)
-            dob[hcols, :] = do
-            rdb[hh] = rd
+            do = dob[hcols, :]
+            rd = rdb[hh]
             dqt = jnp.zeros((HD, BLOCK), F32)
             for slot, col in ((1, col1), (2, col2)):
                 for part in range(2):
@@ -307,24 +332,27 @@
             dot_[hcols, :] = dqt
             return 0
 
-        lax.fori_loop(0, GROUP, one_head, 0)
+        lax.fori_loop(0, GROUP, one_head, 0, unroll=GROUP)
 
     def backward_near(g):
         kt[0] = own[g, 0].T
+        acc[g, 1, 0] = jnp.zeros((BLOCK, HD), F32)
 
         def one_head(r, _):
             hh = g * GROUP + r
             hcols = pl.ds(pl.multiple_of(hh * HD, HD), HD)
             q = qv[:, hcols]
-            do = dob[hcols, :]
-            rd = rdb[hh]
+            do = (dob[hcols, :].astype(F32) * fades[hh]).astype(BF16)
+            rd = rdb[hh] * fades[hh]
+            acc[g, 1, 0, :HALF] += nt(eb[hh, :HALF, :], do)
+            acc[g, 1, 0, HALF:] += nt(eb[hh, HALF:BLOCK, HALF:], do[:, HALF:])
             dqt = dot_[hcols, :] + back_tile(g, 0, None, None, 0, hh, q, do, rd, slice(None))
             late = back_tile(g, 0, None, None, 1, hh, q[HALF:], do[:, HALF:], rd[:, HALF:], slice(HALF, BLOCK))
             dqt = jnp.concatenate([dqt[:, :HALF], dqt[:, HALF:] + late], axis=1)
             dqv[:, hcols] = (dqt * SCALE).T.astype(BF16)
             return 0
 
-        lax.fori_loop(0, GROUP, one_head, 0)
+        lax.fori_loop(0, GROUP, one_head, 0, unroll=GROUP)
 
     give = [
         [
@@ -360,44 +388,48 @@
     def sum_grads(g, part):
         for k in (1, 2, 3):
             give[g][part][k - 1].wait_recv()
-        mine = acc[g, part, 0] * factors[part]
+        mine = None
         back = gs[g][y, part].astype(F32)
         for k in (1, 2, 3):
             came = gr[g][k - 1, part].astype(F32)
             inside = y + k < ROW
-            mine = mine + jnp.where(inside, came, 0.0)
+            kept = jnp.where(inside, came, 0.0)
+            mine = kept if mine is None else mine + kept
             back = back + jnp.where(inside, 0.0, came)
         gxs[g, part] = back.astype(BF16)
         give_back[g][part].start()
-        acc[g, part, 0] = mine
+        acc[g, part, 1] = mine
 
     outs = []
 
     def finish_grads(g, part):
         give_back[g][part].wait_recv()
-        dkv_out[g, part] = (acc[g, part, 0] + gxr[g, part].astype(F32)).astype(BF16)
+        total = acc[g, part, 0] * factors[part] + acc[g, part, 1] + gxr[g, part].astype(F32)
+        dkv_out[g, part] = total.astype(BF16)
         ref = (dk_hbm, dv_hbm)[part]
         cp = pltpu.make_async_copy(dkv_out.at[g, part], ref.at[:, pl.ds(g * HD, HD)], osem.at[2 * g + part])
         cp.start()
         outs.append(cp)
 
     for g in range(KV):
+        value_far(g)
+        send_grads(g, 1)
+    for g in range(KV):
         backward_far(g)
-        for part in (1, 0):
-            send_grads(g, part)
-    for g in range(KV):
-        backward_near(g)
+        send_grads(g, 0)
+    sum_grads(0, 1)
+    backward_near(0)
+    sum_grads(1, 1)
+    backward_near(1)
     cp = pltpu.make_async_copy(dqv, dq_hbm, osem.at[4])
     cp.start()
     outs.append(cp)
+    sum_grads(0, 0)
     for j in range(CUTS):
         project(other_core, j, to_core(1, j))
         p_core[1][j].start()
-    for part in (1, 0):
-        sum_grads(0, part)
     for j in range(CUTS):
         project(head, j, keep(j))
-    sum_grads(1, 1)
     for j in range(CUTS):
         p_core[1][j].wait_recv()
         p_chip[j].wait()
@@ -406,9 +438,8 @@
         cp.start()
         outs.append(cp)
     sum_grads(1, 0)
-    for g in range(KV):
-        for part in (1, 0):
-            finish_grads(g, part)
+    for g, part in ((0, 1), (1, 1), (0, 0), (1, 0)):
+        finish_grads(g, part)
 
     og_core.wait_send()
     for i in range(OG_CUTS):
@@ -478,7 +509,7 @@
             vm((BLOCK, WIDTH), BF16),
             vm((KV * GROUP, 1, BLOCK), F32),
             vm((KV * GROUP, 3 * BLOCK, BLOCK), BF16),
-            vm((3 * BLOCK, BLOCK), F32),
+            vm((2 * BLOCK, BLOCK), F32),
             vm((KV, 2, 3, BLOCK, HD), F32),
             vm((ROW, 2, BLOCK, HD), BF16),
             vm((ROW, 2, BLOCK, HD), BF16),
@@ -494,6 +525,9 @@
             vm((BLOCK, WIDTH), BF16),
             vm((KV, 2, BLOCK, HD), BF16),
             vm((WIDTH, BLOCK), BF16),
+            vm((KV * GROUP, 1, BLOCK), F32),
+            vm((KV * GROUP, 1, BLOCK), F32),
+            vm((KV * GROUP, 1, BLOCK), F32),
             vm((KV * GROUP, 1, BLOCK), F32),
             dma((7,)), dma((5 + CUTS,)),
             dma((KV,)), dma((KV,)), dma((KV, 3)), dma((KV, 3)),

time: 93.8 us -> 91.2 us (0.972); the launches traced: 92.3 us -> 91 us
  Pallas kernels: 91.7 us -> 90.2 us
    pallas_call x1, Pallas kernels: 89 us -> 87.6 us  [local(): pl.pallas_call(kernel, out_shape=shapes, in_specs=[pl.BlockSpec(memory_sp...]
where the time goes in v2:
time: 91.2 us; the launch traced here: 91 us
  Pallas kernels  90.2 us (99%)
    pallas_call x1, Pallas kernels, local(): pl.pallas_call(kernel, out_shape=shapes, in_specs=[pl.BlockSpec(memory_sp...  87.6 us
    pallas_call x1, Pallas kernels, local(): pl.pallas_call(mover, out_shape=shapes, in_specs=[anyspec] * 4, out_specs...  2.63 us

profile of v2, /device:TPU:1, one launch (start us, length us, event | category | flops | bytes accessed | tf_op | source)
XLA Modules:
  0.0 91.0 jit_solution(15880448461301115367)
XLA Ops:
  0.6 87.6 %layer.1 = (bf16[512,1024]{1,0:T(8,128)(2,1)}, bf16[512,1024]{1,0:T(8,128)(2,1)}, bf16[512,256]{1,0:T(8,128)(2,1)}, bf16[512,256]{1,0:T(8,128)(2,1)}) custom-call(s32[1,3]{1,0:T(1,128)} %sel.1, bf16[512,1024]{1,0:T(8,128)(2,1)} %q_hbm.1, bf16[512,256]{1,0:T(8,128)(2,1)} %k_hbm.1, bf16[512,256]{1,0:T(8,128)(2,1)} %v_hbm.1, bf16[1024,4096]{1,0:T(8,128)(2,1)} %w_hbm.1, ...), custom_call_target="tpu_custom_call" | custom-call | flops 17999998976 | bytes 16777216 | tf_op jit(solution)/shard_map/layer/pallas_call | solution.py:493
  88.2 2.6 %move.1 = (bf16[512,1024]{1,0:T(8,128)(2,1)}, bf16[512,1024]{1,0:T(8,128)(2,1)}, bf16[512,256]{1,0:T(8,128)(2,1)}, bf16[512,256]{1,0:T(8,128)(2,1)}) custom-call(bf16[512,1024]{1,0:T(8,128)(2,1)} %get-tuple-element.8.refs_0_, bf16[512,1024]{1,0:T(8,128)(2,1)} %get-tuple-element.9.refs_1_, bf16[512,256]{1,0:T(8,128)(2,1)} %get-tuple-element.10.refs_2_, ...), custom_call_target="tpu_custom_call" | custom-call | tf_op jit(solution)/shard_map/move/pallas_call | solution.py:544

commit v3 on v2

--- a/solution.py
+++ b/solution.py
@@ -38,11 +38,11 @@
 def kernel(
     sel, q_hbm, k_hbm, v_hbm, w_hbm, og_hbm,
     proj_hbm, dq_hbm, dk_hbm, dv_hbm,
-    own, win0, win1, vt, kt, qv, wv, ogb, dot_, ot, ob, rl, eb, sb, acc,
+    own, wink0, winv0, wink1, winv1, vt, kt, qv, wv, ogb, dot_, ot, ob, rl, eb, sb, acc,
     gs0, gs1, gr0, gr1, gxs, gxr, pcs, pcr, pxs, pxr, pown, dqv, dkv_out, dob, rdb, top0, total0, fades,
     lsem, osem, xs, xr, ds_, dr, ocs, ocr, oxs, oxr, ofs, ofr, pcss, pcrs, pxss, pxrs, bds, bdr, bxs, bxr,
 ):
-    win = (win0, win1)
+    win = ((wink0, winv0), (wink1, winv1))
     gs = (gs0, gs1)
     gr = (gr0, gr1)
     ctx = lax.axis_index("ctx")
@@ -91,24 +91,39 @@
         pl.semaphore_signal(barrier, inc=1, device_id=(c, h), device_id_type=MESH)
     pl.semaphore_wait(barrier, 7)
 
-    cross = [
-        remote(own.at[g], win[g].at[y], xs.at[g], xr.at[g], following, head) for g in range(KV)
-    ]
-    serve_own = [
-        [remote(own.at[g], win[g].at[y], ds_.at[g, k - 1], dr.at[g, k - 1], peer(k), head) for k in (1, 2, 3)]
-        for g in range(KV)
-    ]
-    serve_prev = [
-        [remote(win[g].at[y], win[g].at[y], ds_.at[g, k - 1], dr.at[g, k - 1], peer(k), head) for k in (1, 2, 3)]
-        for g in range(KV)
-    ]
-    for g in range(KV):
-        kv_in[g][0].wait()
-        kv_in[g][1].wait()
-        cross[g].start()
-        if g == 0:
-            for k in (1, 3, 2):
-                pl.when(y + k < ROW)(serve_own[g][k - 1].start)
+    pieces = [(g, part) for part in range(2) for g in range(KV)]
+    cross = {
+        (g, p): remote(own.at[g, p], win[g][p].at[y], xs.at[g, p], xr.at[g, p], following, head) for g, p in pieces
+    }
+    serve_own = {
+        (g, p, k): remote(own.at[g, p], win[g][p].at[y], ds_.at[g, p, k - 1], dr.at[g, p, k - 1], peer(k), head)
+        for g, p in pieces
+        for k in (1, 2, 3)
+    }
+    serve_prev = {
+        (g, p, k): remote(win[g][p].at[y], win[g][p].at[y], ds_.at[g, p, k - 1], dr.at[g, p, k - 1], peer(k), head)
+        for g, p in pieces
+        for k in (1, 2, 3)
+    }
+
+    def start_own(g, p):
+        for k in (1, 3, 2):
+            pl.when(y + k < ROW)(serve_own[g, p, k].start)
+
+    def pass_on(g, p):
+        cross[g, p].wait_recv()
+        for k in (3, 1, 2):
+            pl.when(y + k >= ROW)(serve_prev[g, p, k].start)
+
+    def arrived(g, p):
+        for k in (1, 2, 3):
+            serve_own[g, p, k].wait_recv()
+
+    for g, p in pieces:
+        kv_in[g][p].wait()
+        cross[g, p].start()
+        if p == 0:
+            start_own(g, p)
 
     og_in.wait()
     og_core = remote(ogb.at[head], ogb.at[head], ocs.at[0], ocr.at[0], ctx, other_core)
@@ -138,16 +153,14 @@
     w_in.wait()
     grad_block(head, True)
 
-    for g in range(KV):
-        cross[g].wait_recv()
-        for k in (3, 1, 2):
-            pl.when(y + k >= ROW)(serve_prev[g][k - 1].start)
-        if g == 0:
-            for k in (1, 3, 2):
-                pl.when(y + k < ROW)(serve_own[1][k - 1].start)
-        else:
-            for i in range(OG_CUTS):
-                og_chip[i].start()
+    pass_on(0, 0)
+    pass_on(1, 0)
+    start_own(0, 1)
+    pass_on(0, 1)
+    start_own(1, 1)
+    pass_on(1, 1)
+    for i in range(OG_CUTS):
+        og_chip[i].start()
     og_core.wait_recv()
     grad_block(other_core, False)
 
@@ -196,10 +209,8 @@
 
         lax.fori_loop(0, GROUP, one_head, 0)
 
-    def forward_far(g):
+    def scores_far(g):
         w_ = win[g]
-        vt[1] = w_[col1, 1].T
-        vt[2] = w_[col2, 1].T
 
         def one_head(r, _):
             hh = g * GROUP + r
@@ -209,39 +220,51 @@
             top = first_top
             for j, (col, live) in enumerate(((col1, live1), (col2, live2))):
                 for half in range(2):
-                    s = nt(w_[col, 0, half * HALF : (half + 1) * HALF], q)
+                    s = nt(w_[0][col, half * HALF : (half + 1) * HALF], q)
                     sb[BLOCK * j + half * HALF : BLOCK * j + (half + 1) * HALF, :] = s
                     top = jnp.maximum(top, jnp.where(live, jnp.max(s, axis=0, keepdims=True), -1e30))
             shift = top * EXP2_SCALE
             fade = jnp.exp2(first_top * EXP2_SCALE - shift)
             total = total0[hh] * fade
-            out = ot[hcols, :] * fade
             for j, live in enumerate((live1, live2)):
                 sh = jnp.where(live, shift, 1e30)
                 for half in range(2):
                     at = BLOCK * j + half * HALF
                     e = jnp.exp2(sb[at : at + HALF, :] * EXP2_SCALE - sh)
                     total = total + jnp.sum(e, axis=0, keepdims=True)
-                    e = e.astype(BF16)
-                    eb[hh, BLOCK + at : BLOCK + at + HALF, :] = e
-                    out = out + nn(vt[j + 1, :, half * HALF : (half + 1) * HALF], e)
-            recip = 1.0 / total
-            rl[hh] = recip
+                    eb[hh, BLOCK + at : BLOCK + at + HALF, :] = e.astype(BF16)
+            rl[hh] = 1.0 / total
             fades[hh] = fade
-            out = out * recip
+            return 0
+
+        lax.fori_loop(0, GROUP, one_head, 0)
+
+    def values_far(g):
+        w_ = win[g]
+        vt[1] = w_[1][col1].T
+        vt[2] = w_[1][col2].T
+
+        def one_head(r, _):
+            hh = g * GROUP + r
+            hcols = pl.ds(pl.multiple_of(hh * HD, HD), HD)
+            out = ot[hcols, :] * fades[hh]
+            out = out + nn(vt[1], eb[hh, BLOCK : 2 * BLOCK, :]) + nn(vt[2], eb[hh, 2 * BLOCK :, :])
+            out = out * rl[hh]
             ot[hcols, :] = out
             ob[:, hcols] = out.T.astype(BF16)
             return 0
 
-        lax.fori_loop(0, GROUP, one_head, 0)
+        lax.fori_loop(0, GROUP, one_head, 0, unroll=2)
 
     q_in.wait()
     for g in range(KV):
         forward_near(g)
     for g in range(KV):
-        for k in (1, 2, 3):
-            serve_own[g][k - 1].wait_recv()
-        forward_far(g)
+        arrived(g, 0)
+        scores_far(g)
+    for g in range(KV):
+        arrived(g, 1)
+        values_far(g)
 
     def project(block, cut, put):
         def step(i, _):
@@ -295,7 +318,7 @@
     def back_tile(g, slot, w_, col, part, hh, q, do, rd, span):
         keys_at = slice(part * HALF, (part + 1) * HALF)
         e = eb[hh, slot * BLOCK + part * HALF : slot * BLOCK + (part + 1) * HALF, span]
-        v = own[g, 1, keys_at] if slot == 0 else w_[col, 1, keys_at]
+        v = own[g, 1, keys_at] if slot == 0 else w_[1][col, keys_at]
         dp = nn(v, do)
         dsv = (e.astype(F32) * (dp - rd)).astype(BF16)
         acc[g, 0, slot, keys_at] += nn(dsv, q)
@@ -315,8 +338,8 @@
 
     def backward_far(g):
         w_ = win[g]
-        kt[1] = w_[col1, 0].T
-        kt[2] = w_[col2, 0].T
+        kt[1] = w_[0][col1].T
+        kt[2] = w_[0][col2].T
         acc[g, 0] = jnp.zeros(acc.shape[2:], F32)
 
         def one_head(r, _):
@@ -449,10 +472,10 @@
         for j in range(CUTS):
             p_core[i][j].wait_send()
     for g in range(KV):
-        cross[g].wait_send()
-        for k in (1, 2, 3):
-            serve_own[g][k - 1].wait_send()
         for part in range(2):
+            cross[g, part].wait_send()
+            for k in (1, 2, 3):
+                serve_own[g, part, k].wait_send()
             give_back[g][part].wait_send()
             for k in (1, 2, 3):
                 give[g][part][k - 1].wait_send()
@@ -497,8 +520,10 @@
         out_specs=(anyspec,) * 4,
         scratch_shapes=[
             vm((KV, 2, BLOCK, HD), BF16),
-            vm((ROW, 2, BLOCK, HD), BF16),
-            vm((ROW, 2, BLOCK, HD), BF16),
+            vm((ROW, BLOCK, HD), BF16),
+            vm((ROW, BLOCK, HD), BF16),
+            vm((ROW, BLOCK, HD), BF16),
+            vm((ROW, BLOCK, HD), BF16),
             vm((3, HD, BLOCK), BF16),
             vm((3, HD, BLOCK), BF16),
             vm((BLOCK, WIDTH), BF16),
@@ -530,7 +555,7 @@
             vm((KV * GROUP, 1, BLOCK), F32),
             vm((KV * GROUP, 1, BLOCK), F32),
             dma((7,)), dma((5 + CUTS,)),
-            dma((KV,)), dma((KV,)), dma((KV, 3)), dma((KV, 3)),
+            dma((KV, 2)), dma((KV, 2)), dma((KV, 2, 3)), dma((KV, 2, 3)),
             dma((1,)), dma((1,)), dma((OG_CUTS,)), dma((OG_CUTS,)), dma((OG_CUTS,)), dma((OG_CUTS,)),
             dma((2, CUTS)), dma((2, CUTS)), dma((CUTS,)), dma((CUTS,)),
             dma((KV, 2, 3)), dma((KV, 2, 3)), dma((KV, 2)), dma((KV, 2)),

time: 91.2 us -> 89 us (0.976)
  Pallas kernels: 90.2 us -> 88 us
    pallas_call x1, Pallas kernels: 87.6 us -> 85.3 us  [local(): pl.pallas_call(kernel, out_shape=shapes, in_specs=[pl.BlockSpec(memory_sp...]
where the time goes in v3:
time: 89 us; the launch traced here: 88.8 us
  Pallas kernels  88 us (99%)
    pallas_call x1, Pallas kernels, local(): pl.pallas_call(kernel, out_shape=shapes, in_specs=[pl.BlockSpec(memory_sp...  85.3 us
    pallas_call x1, Pallas kernels, local(): pl.pallas_call(mover, out_shape=shapes, in_specs=[anyspec] * 4, out_specs...  2.63 us

profile of v3, /device:TPU:1, one launch (start us, length us, event | category | flops | bytes accessed | tf_op | source)
XLA Modules:
  0.0 88.8 jit_solution(9891848693743878520)
XLA Ops:
  0.6 85.3 %layer.1 = (bf16[512,1024]{1,0:T(8,128)(2,1)}, bf16[512,1024]{1,0:T(8,128)(2,1)}, bf16[512,256]{1,0:T(8,128)(2,1)}, bf16[512,256]{1,0:T(8,128)(2,1)}) custom-call(s32[1,3]{1,0:T(1,128)} %sel.1, bf16[512,1024]{1,0:T(8,128)(2,1)} %q_hbm.1, bf16[512,256]{1,0:T(8,128)(2,1)} %k_hbm.1, bf16[512,256]{1,0:T(8,128)(2,1)} %v_hbm.1, bf16[1024,4096]{1,0:T(8,128)(2,1)} %w_hbm.1, ...), custom_call_target="tpu_custom_call" | custom-call | flops 17999998976 | bytes 16777216 | tf_op jit(solution)/shard_map/layer/pallas_call | solution.py:516
  86.0 2.6 %move.1 = (bf16[512,1024]{1,0:T(8,128)(2,1)}, bf16[512,1024]{1,0:T(8,128)(2,1)}, bf16[512,256]{1,0:T(8,128)(2,1)}, bf16[512,256]{1,0:T(8,128)(2,1)}) custom-call(bf16[512,1024]{1,0:T(8,128)(2,1)} %get-tuple-element.8.refs_0_, bf16[512,1024]{1,0:T(8,128)(2,1)} %get-tuple-element.9.refs_1_, bf16[512,256]{1,0:T(8,128)(2,1)} %get-tuple-element.10.refs_2_, ...), custom_call_target="tpu_custom_call" | custom-call | tf_op jit(solution)/shard_map/move/pallas_call | solution.py:569

commit v4 on v3

--- a/solution.py
+++ b/solution.py
@@ -39,7 +39,7 @@
     sel, q_hbm, k_hbm, v_hbm, w_hbm, og_hbm,
     proj_hbm, dq_hbm, dk_hbm, dv_hbm,
     own, wink0, winv0, wink1, winv1, vt, kt, qv, wv, ogb, dot_, ot, ob, rl, eb, sb, acc,
-    gs0, gs1, gr0, gr1, gxs, gxr, pcs, pcr, pxs, pxr, pown, dqv, dkv_out, dob, rdb, top0, total0, fades,
+    gs0, gs1, gr0, gr1, gxs, gxr, pcs, pcr, pxs, pxr, pown, dqv, dkv_out, dob, rdb, top0, total0, fades, pdiag,
     lsem, osem, xs, xr, ds_, dr, ocs, ocr, oxs, oxr, ofs, ofr, pcss, pcrs, pxss, pxrs, bds, bdr, bxs, bxr,
 ):
     win = ((wink0, winv0), (wink1, winv1))
@@ -262,28 +262,40 @@
     for g in range(KV):
         arrived(g, 0)
         scores_far(g)
-    for g in range(KV):
-        arrived(g, 1)
-        values_far(g)
-
-    def project(block, cut, put):
+    def project(block, cut, put, rows=slice(None)):
         def step(i, _):
             n0 = pl.multiple_of(i * 256, 256)
             cols = pl.ds(pl.multiple_of(block * WIDTH + cut * CUT + n0, 256), 256)
-            put(pl.ds(n0, 256), nn(ob[...], wv[:, cols]))
+            put(pl.ds(n0, 256), nn(ob[:, rows], wv[rows, cols]))
             return 0
 
         lax.fori_loop(0, CUT // 256, step, 0)
+
+    def hold(ref, cut):
+        def put(cols, val):
+            ref[cut, :, cols] = val
+
+        return put
+
+    early = slice(0, GROUP * HD)
+    late = slice(GROUP * HD, WIDTH)
+    arrived(0, 1)
+    values_far(0)
+    for j in range(CUTS):
+        project(diagonal, j, hold(pdiag, j), early)
+        project(other_chip, j, hold(pown, j), early)
+    arrived(1, 1)
+    values_far(1)
 
     def to_core(slot, cut):
         def put(cols, val):
-            pcs[slot, cut, :, cols] = val.astype(BF16)
+            pcs[slot, cut, :, cols] = (val + pdiag[cut, :, cols] if slot == 0 else val).astype(BF16)
 
         return put
 
     def to_chip(cut):
         def put(cols, val):
-            pxs[cut, :, cols] = (val + pcr[0, cut, :, cols].astype(F32)).astype(BF16)
+            pxs[cut, :, cols] = (val + pown[cut, :, cols] + pcr[0, cut, :, cols].astype(F32)).astype(BF16)
 
         return put
 
@@ -298,13 +310,13 @@
         for i in range(2)
     ]
     p_chip = [remote(pxs.at[j], pxr.at[j], pxss.at[j], pxrs.at[j], ctx, other_chip) for j in range(CUTS)]
-    project(diagonal, 0, to_core(0, 0))
+    project(diagonal, 0, to_core(0, 0), late)
     p_core[0][0].start()
-    project(diagonal, 1, to_core(0, 1))
+    project(diagonal, 1, to_core(0, 1), late)
     p_core[0][1].start()
     for j in range(CUTS):
         p_core[0][j].wait_recv()
-        project(other_chip, j, to_chip(j))
+        project(other_chip, j, to_chip(j), late)
         p_chip[j].start()
         if j == 0:
             for i in range(OG_CUTS):
@@ -554,6 +566,7 @@
             vm((KV * GROUP, 1, BLOCK), F32),
             vm((KV * GROUP, 1, BLOCK), F32),
             vm((KV * GROUP, 1, BLOCK), F32),
+            vm((CUTS, BLOCK, CUT), F32),
             dma((7,)), dma((5 + CUTS,)),
             dma((KV, 2)), dma((KV, 2)), dma((KV, 2, 3)), dma((KV, 2, 3)),
             dma((1,)), dma((1,)), dma((OG_CUTS,)), dma((OG_CUTS,)), dma((OG_CUTS,)), dma((OG_CUTS,)),

time: 89 us -> 86.8 us (0.975)
  Pallas kernels: 88 us -> 85.8 us
    pallas_call x1, Pallas kernels: 85.3 us -> 83.2 us  [local(): pl.pallas_call(kernel, out_shape=shapes, in_specs=[pl.BlockSpec(memory_sp...]
where the time goes in v4:
time: 86.8 us; the launch traced here: 86.7 us
  Pallas kernels  85.8 us (99%)
    pallas_call x1, Pallas kernels, local(): pl.pallas_call(kernel, out_shape=shapes, in_specs=[pl.BlockSpec(memory_sp...  83.2 us
    pallas_call x1, Pallas kernels, local(): pl.pallas_call(mover, out_shape=shapes, in_specs=[anyspec] * 4, out_specs...  2.63 us

profile of v4, /device:TPU:1, one launch (start us, length us, event | category | flops | bytes accessed | tf_op | source)
XLA Modules:
  0.0 86.7 jit_solution(16352121525135460034)
XLA Ops:
  0.6 83.2 %layer.1 = (bf16[512,1024]{1,0:T(8,128)(2,1)}, bf16[512,1024]{1,0:T(8,128)(2,1)}, bf16[512,256]{1,0:T(8,128)(2,1)}, bf16[512,256]{1,0:T(8,128)(2,1)}) custom-call(s32[1,3]{1,0:T(1,128)} %sel.1, bf16[512,1024]{1,0:T(8,128)(2,1)} %q_hbm.1, bf16[512,256]{1,0:T(8,128)(2,1)} %k_hbm.1, bf16[512,256]{1,0:T(8,128)(2,1)} %v_hbm.1, bf16[1024,4096]{1,0:T(8,128)(2,1)} %w_hbm.1, ...), custom_call_target="tpu_custom_call" | custom-call | flops 17999998976 | bytes 16777216 | tf_op jit(solution)/shard_map/layer/pallas_call | solution.py:528
  83.8 2.6 %move.1 = (bf16[512,1024]{1,0:T(8,128)(2,1)}, bf16[512,1024]{1,0:T(8,128)(2,1)}, bf16[512,256]{1,0:T(8,128)(2,1)}, bf16[512,256]{1,0:T(8,128)(2,1)}) custom-call(bf16[512,1024]{1,0:T(8,128)(2,1)} %get-tuple-element.8.refs_0_, bf16[512,1024]{1,0:T(8,128)(2,1)} %get-tuple-element.9.refs_1_, bf16[512,256]{1,0:T(8,128)(2,1)} %get-tuple-element.10.refs_2_, ...), custom_call_target="tpu_custom_call" | custom-call | tf_op jit(solution)/shard_map/move/pallas_call | solution.py:582

commit v5 on v4

--- a/solution.py
+++ b/solution.py
@@ -465,6 +465,7 @@
         p_core[1][j].start()
     for j in range(CUTS):
         project(head, j, keep(j))
+    sum_grads(1, 0)
     for j in range(CUTS):
         p_core[1][j].wait_recv()
         p_chip[j].wait()
@@ -472,7 +473,6 @@
         cp = pltpu.make_async_copy(pxs.at[j], proj_hbm.at[:, pl.ds(j * CUT, CUT)], osem.at[5 + j])
         cp.start()
         outs.append(cp)
-    sum_grads(1, 0)
     for g, part in ((0, 1), (1, 1), (0, 0), (1, 0)):
         finish_grads(g, part)
 

time: 86.8 us -> 86.2 us (level); the launches traced: 86.7 us -> 84.9 us
  Pallas kernels: 85.8 us -> 84.1 us
    pallas_call x1, Pallas kernels: 83.2 us -> 81.4 us  [local(): pl.pallas_call(kernel, out_shape=shapes, in_specs=[pl.BlockSpec(memory_sp...]
where the time goes in v5:
time: 86.2 us; the launch traced here: 84.9 us
  Pallas kernels  84.1 us (98%)
    pallas_call x1, Pallas kernels, local(): pl.pallas_call(kernel, out_shape=shapes, in_specs=[pl.BlockSpec(memory_sp...  81.4 us
    pallas_call x1, Pallas kernels, local(): pl.pallas_call(mover, out_shape=shapes, in_specs=[anyspec] * 4, out_specs...  2.63 us

profile of v5, /device:TPU:1, one launch (start us, length us, event | category | flops | bytes accessed | tf_op | source)
XLA Modules:
  0.0 84.9 jit_solution(1634412998010260324)
XLA Ops:
  0.6 81.4 %layer.1 = (bf16[512,1024]{1,0:T(8,128)(2,1)}, bf16[512,1024]{1,0:T(8,128)(2,1)}, bf16[512,256]{1,0:T(8,128)(2,1)}, bf16[512,256]{1,0:T(8,128)(2,1)}) custom-call(s32[1,3]{1,0:T(1,128)} %sel.1, bf16[512,1024]{1,0:T(8,128)(2,1)} %q_hbm.1, bf16[512,256]{1,0:T(8,128)(2,1)} %k_hbm.1, bf16[512,256]{1,0:T(8,128)(2,1)} %v_hbm.1, bf16[1024,4096]{1,0:T(8,128)(2,1)} %w_hbm.1, ...), custom_call_target="tpu_custom_call" | custom-call | flops 17999998976 | bytes 16777216 | tf_op jit(solution)/shard_map/layer/pallas_call | solution.py:528
  82.1 2.6 %move.1 = (bf16[512,1024]{1,0:T(8,128)(2,1)}, bf16[512,1024]{1,0:T(8,128)(2,1)}, bf16[512,256]{1,0:T(8,128)(2,1)}, bf16[512,256]{1,0:T(8,128)(2,1)}) custom-call(bf16[512,1024]{1,0:T(8,128)(2,1)} %get-tuple-element.8.refs_0_, bf16[512,1024]{1,0:T(8,128)(2,1)} %get-tuple-element.9.refs_1_, bf16[512,256]{1,0:T(8,128)(2,1)} %get-tuple-element.10.refs_2_, ...), custom_call_target="tpu_custom_call" | custom-call | tf_op jit(solution)/shard_map/move/pallas_call | solution.py:582

commit v6 on v5

--- a/solution.py
+++ b/solution.py
@@ -139,7 +139,7 @@
             remote(ogb.at[other_chip, rows], ogb.at[other_chip, rows], ofs.at[i], ofr.at[i], ctx, other_core)
         )
 
-    def grad_block(block, first):
+    def grad_block(block, first, start=0, stop=WIDTH // 256):
         cols = pl.ds(pl.multiple_of(block * WIDTH, WIDTH), WIDTH)
 
         def step(i, _):
@@ -148,7 +148,7 @@
             dot_[rows, :] = part if first else dot_[rows, :] + part
             return 0
 
-        lax.fori_loop(0, WIDTH // 256, step, 0)
+        lax.fori_loop(start, stop, step, 0)
 
     w_in.wait()
     grad_block(head, True)
@@ -322,10 +322,13 @@
             for i in range(OG_CUTS):
                 og_chip[i].wait_recv()
                 og_pass[i].start()
-    grad_block(other_chip, False)
-    for i in range(OG_CUTS):
-        og_pass[i].wait_recv()
-    grad_block(diagonal, False)
+    def grad_rest(g):
+        steps = GROUP * HD // 256
+        grad_block(other_chip, False, g * steps, (g + 1) * steps)
+        if g == 0:
+            for i in range(OG_CUTS):
+                og_pass[i].wait_recv()
+        grad_block(diagonal, False, g * steps, (g + 1) * steps)
 
     def back_tile(g, slot, w_, col, part, hh, q, do, rd, span):
         keys_at = slice(part * HALF, (part + 1) * HALF)
@@ -447,6 +450,7 @@
         outs.append(cp)
 
     for g in range(KV):
+        grad_rest(g)
         value_far(g)
         send_grads(g, 1)
     for g in range(KV):

time: 86.2 us -> 85.9 us (level); the launches traced: 84.9 us -> 85.8 us
  Pallas kernels: 84.1 us -> 85 us
    pallas_call x1, Pallas kernels: 81.4 us -> 82.4 us  [local(): pl.pallas_call(kernel, out_shape=shapes, in_specs=[pl.BlockSpec(memory_sp...]
where the time goes in v6:
time: 85.9 us; the launch traced here: 85.8 us
  Pallas kernels  85 us (99%)
    pallas_call x1, Pallas kernels, local(): pl.pallas_call(kernel, out_shape=shapes, in_specs=[pl.BlockSpec(memory_sp...  82.4 us
    pallas_call x1, Pallas kernels, local(): pl.pallas_call(mover, out_shape=shapes, in_specs=[anyspec] * 4, out_specs...  2.63 us

profile of v6, /device:TPU:1, one launch (start us, length us, event | category | flops | bytes accessed | tf_op | source)
XLA Modules:
  0.0 85.8 jit_solution(16075041764331473039)
XLA Ops:
  0.6 82.4 %layer.1 = (bf16[512,1024]{1,0:T(8,128)(2,1)}, bf16[512,1024]{1,0:T(8,128)(2,1)}, bf16[512,256]{1,0:T(8,128)(2,1)}, bf16[512,256]{1,0:T(8,128)(2,1)}) custom-call(s32[1,3]{1,0:T(1,128)} %sel.1, bf16[512,1024]{1,0:T(8,128)(2,1)} %q_hbm.1, bf16[512,256]{1,0:T(8,128)(2,1)} %k_hbm.1, bf16[512,256]{1,0:T(8,128)(2,1)} %v_hbm.1, bf16[1024,4096]{1,0:T(8,128)(2,1)} %w_hbm.1, ...), custom_call_target="tpu_custom_call" | custom-call | flops 17999998976 | bytes 16777216 | tf_op jit(solution)/shard_map/layer/pallas_call | solution.py:532
  83.0 2.6 %move.1 = (bf16[512,1024]{1,0:T(8,128)(2,1)}, bf16[512,1024]{1,0:T(8,128)(2,1)}, bf16[512,256]{1,0:T(8,128)(2,1)}, bf16[512,256]{1,0:T(8,128)(2,1)}) custom-call(bf16[512,1024]{1,0:T(8,128)(2,1)} %get-tuple-element.8.refs_0_, bf16[512,1024]{1,0:T(8,128)(2,1)} %get-tuple-element.9.refs_1_, bf16[512,256]{1,0:T(8,128)(2,1)} %get-tuple-element.10.refs_2_, ...), custom_call_target="tpu_custom_call" | custom-call | tf_op jit(solution)/shard_map/move/pallas_call | solution.py:586
